TPU v7x, 32 devices: a whole 2x2x4 slice. The times are simulated.
32 devices in a mesh: grp: 2 (over y), wide: 4 (over z), tp: 4 (over x, core).
Axes of the slice: x: 2, y: 2, z: 4, core: 2. Of those that a mesh axis runs over, the one named last changes fastest.
Arguments:
- hidden: bfloat16 [24, 8192], P('grp', 'wide'), parts along dimension 0, may hold values from -6 to 6
- norm_gain: bfloat16 [8192], P('wide'), may hold values from 0.5 to 2
- query_key_value_weight: bfloat16 [8192, 10240], P('wide', 'tp'), may hold values from -0.0625 to 0.0625
- w_out: bfloat16 [8192, 8192], P('tp', 'wide'), may hold values from -0.0625 to 0.0625
- prompt_kv: bfloat16 [16, 512, 2048], P(('grp', 'wide'), None, 'tp'), parts along dimension 0, may hold values from -68 to 68
- kept_rows: int32 [16, 8, 16], P(('grp', 'wide'), 'tp'), parts along dimension 0, may hold values from 0 to 511, as said below
- owners: int32 [16], P('grp'), parts along dimension 0, may hold values from 0 to 3, as said below
- kept_len: int32 [16], P('grp'), parts along dimension 0, may hold values from 1 to 16, 96 in all
Outputs:
- state_out: bfloat16 [24, 8192], P('grp', 'wide'), parts along dimension 0
- attended: bfloat16 [24, 8192], P(('grp', 'wide'), 'tp'), parts along dimension 0
There are 2 independent parts, one for each index of `grp`. A program takes and returns all parts, laid end to end along the dimension named above; an argument that names none is the same for every part. Nothing has to cross between parts.
Inputs may be any that keep to these rules, and one draw needn't show every extreme that they name: The 2 requests of one prefill device go to different owners; every owner receives at most 3 requests, and one owner exactly 3. `kept_rows`: each list holds distinct positions in rising order and ends with the prompt's last position.
All inputs are finite; a program needn't handle non-finite values.
Results may differ from a plain program's by a relative error of at most 0.02.
Values may be sent and summed in bfloat16 or wider, within the bound.
No kernel may reach another device: no remote copies, remote signals or barrier semaphores. Data moves between devices by JAX's collectives and lax.ppermute only.
A program may use at most 64 MiB of HBM per device.

v0:
```python
import math

import jax
import jax.numpy as jnp
from jax import lax
from jax.sharding import PartitionSpec as P

MODEL_WIDTH = 8192
HEAD_WIDTH = 128
QUERY_PER_KEY = 8
STEPS = 2


theta_base = 500000.0
eps_norm = 1e-05


def rotate(vector, position):
    half_dim = vector.shape[-1] // 2
    frequency = theta_base ** (-jnp.arange(half_dim).astype(jnp.float32) / half_dim)
    angles = position.astype(jnp.float32)[:, None, None, None] * frequency
    front_half = vector[..., :half_dim]
    back_half = vector[..., half_dim:]
    cosine = jnp.cos(angles)
    sine_part = jnp.sin(angles)
    return jnp.concatenate(
        [front_half * cosine - back_half * sine_part, back_half * cosine + front_half * sine_part],
        axis=-1,
    )


def slot_table(owners, own_cap):
    request_count = owners.shape[0]
    positions = jnp.arange(request_count, dtype=jnp.int32)
    earlier = (owners[None, :] == owners[:, None]) & (positions[None, :] < positions[:, None])
    order_rank = jnp.sum(earlier.astype(jnp.int32), axis=1)
    return owners * own_cap + order_rank


def attend(queries, kept_keys, kept_values, slot_len, new_keys, new_values):
    score_scale = 1.0 / math.sqrt(queries.shape[-1])
    scores_kept = (
        jnp.einsum("ngqd,nkgd->ngqk", queries, kept_keys, preferred_element_type=jnp.float32)
        * score_scale
    )
    valid = jnp.arange(kept_keys.shape[1], dtype=jnp.int32)[None, :] < slot_len[:, None]
    scores_kept = jnp.where(valid[:, None, None, :], scores_kept, -1e30)
    fresh_keys = jnp.stack(new_keys, axis=1)
    fresh_values = jnp.stack(new_values, axis=1)
    scores_new = (
        jnp.einsum("ngqd,ntgd->ngqt", queries, fresh_keys, preferred_element_type=jnp.float32)
        * score_scale
    )
    highest = jnp.maximum(jnp.max(scores_kept, axis=-1), jnp.max(scores_new, axis=-1))
    weights_kept = jnp.exp(scores_kept - highest[..., None])
    weights_new = jnp.exp(scores_new - highest[..., None])
    denominator = jnp.sum(weights_kept, axis=-1) + jnp.sum(weights_new, axis=-1)
    summed = jnp.einsum(
        "ngqk,nkgd->ngqd",
        weights_kept.astype(jnp.bfloat16),
        kept_values,
        preferred_element_type=jnp.float32,
    )
    summed = summed + jnp.einsum(
        "ngqt,ntgd->ngqd",
        weights_new.astype(jnp.bfloat16),
        fresh_values,
        preferred_element_type=jnp.float32,
    )
    result = (summed / denominator[..., None]).astype(jnp.bfloat16)
    return result.reshape(result.shape[0], -1)


def shards(
    hidden, norm_gain, query_key_value_weight, w_out, prompt_kv, kept_rows, owners, kept_len
):
    wide_count = lax.axis_size("wide")
    owner_index = lax.axis_index("wide")
    own_cap = hidden.shape[0] // wide_count
    heads_local = kept_rows.shape[1]
    request_count = owners.shape[0]
    slot_of = slot_table(owners, own_cap)
    my_slots = owner_index * own_cap + jnp.arange(own_cap, dtype=jnp.int32)
    matches = my_slots[:, None] == slot_of[None, :]
    occupied = jnp.any(matches, axis=1)
    slot_req = jnp.sum(
        jnp.where(matches, jnp.arange(request_count, dtype=jnp.int32)[None, :], 0), axis=1
    )
    slot_len = jnp.sum(jnp.where(matches, kept_len[None, :], 0), axis=1)
    head_blocks = []
    for head_number in range(heads_local):
        head_block = prompt_kv[
            :, :, head_number * 2 * HEAD_WIDTH : (head_number + 1) * 2 * HEAD_WIDTH
        ]
        head_blocks.append(
            jnp.take_along_axis(head_block, kept_rows[:, head_number, :, None], axis=1)
        )
    kept_kv = jnp.concatenate(head_blocks, axis=2)
    collect_block_rows = lax.all_gather(kept_kv, "wide", axis=0, tiled=True)
    request_ids = jnp.arange(collect_block_rows.shape[0], dtype=jnp.int32)
    selector = ((slot_req[:, None] == request_ids[None, :]) & occupied[:, None]).astype(
        jnp.bfloat16
    )
    cache = jnp.einsum(
        "jp,pkc->jkc", selector, collect_block_rows, preferred_element_type=jnp.float32
    ).astype(jnp.bfloat16)
    cache = cache.reshape(own_cap, cache.shape[1], heads_local, 2 * HEAD_WIDTH)
    kept_keys = cache[..., :HEAD_WIDTH]
    kept_values = cache[..., HEAD_WIDTH:]
    state = hidden
    new_keys = []
    new_values = []
    attended = None
    for step_index in range(STEPS):
        state_wide = state.astype(jnp.float32)
        squares = lax.psum(jnp.sum(state_wide * state_wide, axis=1), "wide")
        normalized_input = (
            state_wide
            * lax.rsqrt(squares / MODEL_WIDTH + eps_norm)[:, None]
            * norm_gain.astype(jnp.float32)
        ).astype(jnp.bfloat16)
        projected_rows = lax.psum_scatter(
            jnp.dot(normalized_input, query_key_value_weight, preferred_element_type=jnp.float32),
            "wide",
            scatter_dimension=0,
            tiled=True,
        )
        projected_rows = projected_rows.reshape(own_cap, heads_local, QUERY_PER_KEY + 2, HEAD_WIDTH)
        position = slot_len + step_index
        queries = rotate(projected_rows[:, :, :QUERY_PER_KEY], position).astype(jnp.bfloat16)
        key_step = rotate(projected_rows[:, :, QUERY_PER_KEY : QUERY_PER_KEY + 1], position)[
            :, :, 0
        ].astype(jnp.bfloat16)
        value_step = projected_rows[:, :, QUERY_PER_KEY + 1].astype(jnp.bfloat16)
        new_keys.append(key_step)
        new_values.append(value_step)
        attended = attend(queries, kept_keys, kept_values, slot_len, new_keys, new_values)
        partial_rows = jnp.dot(
            lax.all_gather(attended, "wide", axis=0, tiled=True),
            w_out,
            preferred_element_type=jnp.float32,
        )
        summed = lax.psum(partial_rows, "tp")
        state = (state_wide + summed).astype(jnp.bfloat16)
    return (state, attended)


def solution(mesh):
    in_specs = (
        P("grp", "wide"),
        P("wide"),
        P("wide", "tp"),
        P("tp", "wide"),
        P(("grp", "wide"), None, "tp"),
        P(("grp", "wide"), "tp", None),
        P("grp"),
        P("grp"),
    )
    out_specs = (P("grp", "wide"), P(("grp", "wide"), "tp"))
    return jax.shard_map(shards, mesh=mesh, in_specs=in_specs, out_specs=out_specs, check_vma=False)
```

profile of v0, /device:TPU:0, one launch (start us, length us, event | category | flops | bytes accessed | tf_op | source)
XLA Modules:
  0.0 224.6 jit_solution(16107463521871614594)
XLA Ops:
  7.3 1.0 fusion.6
  8.3 0.7 convert_element_type.134
  9.0 13.4 %psum.28 = f32[12]{0:T(128)S(1)} all-reduce(f32[12]{0:T(128)S(1)} %fusion.6), channel_id=1, replica_groups=mesh['grp'=2,'wide'=4,'tp'=4] {'wide'}, use_global_device_ids=true, to_apply=%region_3.4 | all-reduce | flops 12 | bytes 96 | tf_op jit(solution)/shard_map/psum | solution.py:116
  22.4 6.2 %fusion.17 = f32[12,2560]{1,0:T(8,128)} fusion(bf16[2048,2560]{1,0:T(8,128)(2,1)} %param.12, bf16[12,2048]{1,0:T(8,128)(2,1)} %param.10, f32[2048]{0:T(1024)S(1)} %convert_element_type.134, f32[12]{0:T(128)S(1)} %add_rsqrt_fusion.1), kind=kOutput, calls=%fused_computation.30 | convolution fusion | flops 125927424 | bytes 10666032 | tf_op jit(solution)/shard_map/dot_general | solution.py:123
  29.1 0.7 gather_fusion.1
  29.7 0.7 gather_fusion
  30.5 13.7 %all_gather.9 = bf16[8,16,512]{2,1,0:T(8,128)(2,1)S(1)} all-gather(bf16[2,16,512]{2,1,0:T(8,128)(2,1)S(1)} %pad_maximum_fusion), channel_id=1, replica_groups=mesh['grp'=2,'wide'=4,'tp'=4] {'wide'}, dimensions={0}, use_global_device_ids=true | all-gather | bytes 163840 | tf_op jit(solution)/shard_map/all_gather | solution.py:99
  45.2 0.6 dynamic-slice
  46.6 15.3 %all-reduce.11.cloned.1.call-done = f32[12,2560]{1,0:T(8,128)} async-done(((f32[12,2560]{1,0:T(8,128)}), f32[12,2560]{1,0:T(8,128)}) %all-reduce.11.cloned.1.call-update) | async-done | bytes 122896
  61.9 0.9 constant_dynamic-slice_fusion.1
  63.1 0.3 fusion.70
  64.0 13.1 %all-gather = bf16[4,3,2048]{2,1,0:T(4,128)(2,1)S(1)} all-gather(bf16[1,3,2048]{2,1,0:T(4,128)(2,1)S(1)} %reshape.247), channel_id=1, replica_groups=mesh['grp'=2,'wide'=4,'tp'=4] {'wide'}, dimensions={0}, use_global_device_ids=true | all-gather | bytes 61440 | tf_op jit(solution)/shard_map/all_gather | solution.py:139
  77.1 5.2 %fusion.73 = f32[12,2048]{1,0:T(8,128)} fusion(bf16[12,2048]{1,0:T(8,128)(2,1)S(1)} %reshape.248, bf16[2048,2048]{1,0:T(8,128)(2,1)} %param.13), kind=kOutput, calls=%fused_computation.130 | convolution fusion | flops 100663296 | bytes 8536064 | tf_op jit(solution)/shard_map/dot_general | solution.py:138
  82.4 31.1 %all-reduce.7.cloned.1.call-done = f32[12,2048]{1,0:T(8,128)} async-done(((f32[12,2048]{1,0:T(8,128)}), f32[12,2048]{1,0:T(8,128)}) %all-reduce.7.cloned.1.call-update) | async-done | bytes 98320 | tf_op jit(solution)/shard_map/psum | solution.py:143
  113.6 1.0 fusion.10
  114.6 11.7 %psum.30 = f32[12]{0:T(128)S(1)} all-reduce(f32[12]{0:T(128)S(1)} %get-tuple-element.5), channel_id=1, replica_groups=mesh['grp'=2,'wide'=4,'tp'=4] {'wide'}, use_global_device_ids=true, to_apply=%region_11.13 | all-reduce | flops 12 | bytes 96 | tf_op jit(solution)/shard_map/psum | solution.py:116
  126.3 6.1 %fusion.15 = f32[12,2560]{1,0:T(8,128)} fusion(bf16[2048,2560]{1,0:T(8,128)(2,1)} %param.12, bf16[12,2048]{1,0:T(8,128)(2,1)S(1)} %get-tuple-element.6, f32[12]{0:T(128)S(1)} %add_rsqrt_fusion, f32[2048]{0:T(1024)S(1)} %convert_element_type.134), kind=kOutput, calls=%fused_computation.29 | convolution fusion | flops 125927424 | bytes 10666032 | tf_op jit(solution)/shard_map/dot_general | solution.py:123
  132.6 31.9 %all-reduce.13.cloned.1.call-done = f32[12,2560]{1,0:T(8,128)} async-done(((f32[12,2560]{1,0:T(8,128)}), f32[12,2560]{1,0:T(8,128)}) %all-reduce.13.cloned.1.call-update) | async-done | bytes 122896
  164.6 0.9 constant_dynamic-slice_fusion
  166.9 13.1 %all-gather.1 = bf16[4,3,2048]{2,1,0:T(4,128)(2,1)S(1)} all-gather(bf16[1,3,2048]{2,1,0:T(4,128)(2,1)S(1)} %reshape.249), channel_id=1, replica_groups=mesh['grp'=2,'wide'=4,'tp'=4] {'wide'}, dimensions={0}, use_global_device_ids=true | all-gather | bytes 61440 | tf_op jit(solution)/shard_map/all_gather | solution.py:139
  180.1 5.2 %fusion.74 = f32[12,2048]{1,0:T(8,128)} fusion(bf16[12,2048]{1,0:T(8,128)(2,1)S(1)} %reshape.250, bf16[2048,2048]{1,0:T(8,128)(2,1)} %param.13), kind=kOutput, calls=%fused_computation.131 | convolution fusion | flops 100663296 | bytes 8536064 | tf_op jit(solution)/shard_map/dot_general | solution.py:138
  185.3 0.6 copy.94
  186.0 30.6 %all-reduce.9.cloned.1.call-done = f32[12,2048]{1,0:T(8,128)} async-done(((f32[12,2048]{1,0:T(8,128)}), f32[12,2048]{1,0:T(8,128)}) %all-reduce.9.cloned.1.call-update) | async-done | bytes 98320 | tf_op jit(solution)/shard_map/psum | solution.py:143
  216.6 1.5 fusion.13
  (71 shorter events, 4.0 us)
Async XLA Ops:
  7.2 38.0 %copy-start.5 = (u32[32]{0:T(128)S(1)}, u32[32]{0:T(128)}, u32[]{:S(2)}) copy-start(u32[32]{0:T(128)} %constant.82) | copy-start | bytes 388
  7.2 21.5 %copy-start.2 = (s32[2,2,16]{2,1,0:T(2,128)S(1)}, s32[2,2,16]{2,1,0:T(2,128)}, u32[]{:S(2)}) copy-start(s32[2,2,16]{2,1,0:T(2,128)} %param.15) | copy-start | bytes 772
  7.2 21.6 %copy-start = (bf16[2,512,512]{2,1,0:T(8,128)(2,1)S(1)}, bf16[2,512,512]{2,1,0:T(8,128)(2,1)}, u32[]{:S(2)}) copy-start(bf16[2,512,512]{2,1,0:T(8,128)(2,1)} %param.14) | copy-start | bytes 3145732
  7.2 37.0 %copy-start.4 = (s32[8]{0:T(128)S(1)}, s32[8]{0:T(128)}, u32[]{:S(2)}) copy-start(s32[8]{0:T(128)} %param.16) | copy-start | bytes 100
  7.2 37.4 %copy-start.3 = (s32[8]{0:T(128)S(1)}, s32[8]{0:T(128)}, u32[]{:S(2)}) copy-start(s32[8]{0:T(128)} %param.17) | copy-start | bytes 100
  7.2 54.7 %all-reduce.11.cloned.1.call-start = ((), (), s32[]{:S(2)}) async-start(), calls=%async_computation.2 | async-start | bytes 327680
  28.6 85.0 %copy-start.1 = (bf16[12,2048]{1,0:T(8,128)(2,1)S(1)}, bf16[12,2048]{1,0:T(8,128)(2,1)}, u32[]{:S(2)}) copy-start(bf16[12,2048]{1,0:T(8,128)(2,1)} %param.10) | copy-start | bytes 147460
  28.6 85.0 %all-reduce.7.cloned.1.call-start = ((), (), s32[]{:S(2)}) async-start(), calls=%async_computation | async-start | bytes 262144 | tf_op jit(solution)/shard_map/psum | solution.py:143
  82.4 82.2 %all-reduce.13.cloned.1.call-start = ((), (), s32[]{:S(2)}) async-start(), calls=%async_computation.3 | async-start | bytes 327680
  132.5 84.0 %all-reduce.9.cloned.1.call-start = ((), (), s32[]{:S(2)}) async-start(), calls=%async_computation.1 | async-start | bytes 262144 | tf_op jit(solution)/shard_map/psum | solution.py:143
Sparse Core Ops, SparseCore 0:
  28.8 33.1 all-reduce.10
  82.5 31.0 all-reduce.6
  132.6 31.8 all-reduce.12
  185.5 31.0 all-reduce.8
where the time goes:
time: 225 us
  waiting for transfers between devices  109 us (48%)
  blocking collectives  65.1 us (29%)
  matrix products  24.6 us (11%)
  between operations  14.7 us (7%)
  other arithmetic  6.1 us (3%)
  local copies, waits for them, and re-layouts  4.93 us (2%)
    psum x2, waiting for transfers between devices, shards(): summed = lax.psum(partial_rows, 'tp')  61.8 us
    unnamed x6, waiting for transfers between devices  47.3 us
    all_gather x2, blocking collectives, shards(): lax.all_gather(attended, 'wide', axis=0, tiled=True)  26.3 us
    psum x2, blocking collectives, shards(): squares = lax.psum(jnp.sum(state_wide * state_wide, axis=1), 'wide')  25.1 us
    all_gather x1, blocking collectives, shards(): collect_block_rows = lax.all_gather(kept_kv, 'wide', axis=0, tiled=True)  13.7 us
    dot_general x2, matrix products, shards(): jnp.dot(normalized_input, query_key_value_weight, preferred_element_type=...  12.3 us
    dot_general x2, matrix products, shards(): jnp.dot(lax.all_gather(attended, 'wide', axis=0, tiled=True), w_out, pref...  10.5 us
  transfers between devices with their start and end apart: 4, of which 4 were waited for; matrix products, arithmetic and copies ran while one was open for 2% of the time, Pallas kernels for 0%

commit v1 on v0

v1 whole, which is shorter than its diff:
```python
import math

import jax
import jax.numpy as jnp
from jax import lax
from jax.sharding import PartitionSpec as P

HEAD_WIDTH = 128
QUERY_PER_KEY = 8
STEPS = 2
DIRECT_LIMIT = 8

theta_base = 500000.0
eps_norm = 1e-05


def exchange_sum(partial, axis):
    count = lax.axis_size(axis)
    if count > DIRECT_LIMIT:
        return lax.psum(partial.astype(jnp.float32), axis)
    terms = [partial.astype(jnp.float32)]
    for offset in range(1, count):
        pairs = [(i, i ^ offset) for i in range(count)]
        terms.append(lax.ppermute(partial, axis, pairs).astype(jnp.float32))
    while len(terms) > 1:
        terms = [terms[i] + terms[i + 1] for i in range(0, len(terms), 2)]
    return terms[0]


def exchange_gather(block, axis):
    count = lax.axis_size(axis)
    if count > DIRECT_LIMIT:
        return lax.all_gather(block, axis, axis=0, tiled=True)
    blocks = [block]
    for offset in range(1, count):
        pairs = [(i, i ^ offset) for i in range(count)]
        blocks.append(lax.ppermute(block, axis, pairs))
    return blocks


def rotate(vector, cosine, sine):
    half = vector.shape[-1] // 2
    front, back = vector[..., :half], vector[..., half:]
    return jnp.concatenate([front * cosine - back * sine, back * cosine + front * sine], axis=-1)


def shards(
    hidden, norm_gain, query_key_value_weight, w_out, prompt_kv, kept_rows, owners, kept_len
):
    wide_count = lax.axis_size("wide")
    me = lax.axis_index("wide")
    slots = hidden.shape[0]
    own_cap = slots // wide_count
    model_width = hidden.shape[1] * wide_count
    requests_dev, heads = kept_rows.shape[0], kept_rows.shape[1]
    kept_positions = kept_rows.shape[2]
    requests = owners.shape[0]

    ids = jnp.arange(requests, dtype=jnp.int32)
    earlier = (owners[None, :] == owners[:, None]) & (ids[None, :] < ids[:, None])
    slot_of = owners * own_cap + jnp.sum(earlier.astype(jnp.int32), axis=1)
    matches = jnp.arange(slots, dtype=jnp.int32)[:, None] == slot_of[None, :]
    slot_len = jnp.sum(jnp.where(matches, kept_len[None, :], 0), axis=1)

    length = prompt_kv.shape[1]
    pick = (
        kept_rows[..., None] == jnp.arange(length, dtype=jnp.int32)
    ).astype(jnp.bfloat16)
    kept = jnp.einsum(
        "rgkp,rpgc->rgkc",
        pick,
        prompt_kv.reshape(requests_dev, length, heads, 2 * HEAD_WIDTH),
        preferred_element_type=jnp.float32,
    ).astype(jnp.bfloat16)
    blocks = exchange_gather(kept, "wide")
    if isinstance(blocks, list):
        cache = 0.0
        for offset, block in enumerate(blocks):
            source = me ^ offset
            columns = lax.dynamic_slice_in_dim(matches, source * requests_dev, requests_dev, axis=1)
            cache = cache + jnp.einsum(
                "sr,rgkc->sgkc",
                columns.astype(jnp.bfloat16),
                block,
                preferred_element_type=jnp.float32,
            )
        cache = cache.astype(jnp.bfloat16)
    else:
        cache = jnp.einsum(
            "sr,rgkc->sgkc",
            matches.astype(jnp.bfloat16),
            blocks,
            preferred_element_type=jnp.float32,
        ).astype(jnp.bfloat16)
    keys, values = cache[..., :HEAD_WIDTH], cache[..., HEAD_WIDTH:]
    valid = jnp.arange(kept_positions, dtype=jnp.int32)[None, :] < slot_len[:, None]
    score_scale = 1.0 / math.sqrt(HEAD_WIDTH)

    half = HEAD_WIDTH // 2
    frequency = theta_base ** (-jnp.arange(half).astype(jnp.float32) / half)
    gain = norm_gain.astype(jnp.float32)
    state = hidden
    new_keys, new_values = [], []
    attended = None
    for step in range(STEPS):
        state_wide = state.astype(jnp.float32)
        squares = jnp.sum(state_wide * state_wide, axis=1)
        high = squares.astype(jnp.bfloat16)
        low = (squares - high.astype(jnp.float32)).astype(jnp.bfloat16)
        product = jnp.dot(
            (state_wide * gain).astype(jnp.bfloat16),
            query_key_value_weight,
            preferred_element_type=jnp.float32,
        ).astype(jnp.bfloat16)
        tail = jnp.concatenate(
            [jnp.broadcast_to(high[:, None], (slots, 64)), jnp.broadcast_to(low[:, None], (slots, 64))],
            axis=1,
        )
        total = exchange_sum(jnp.concatenate([product, tail], axis=1), "wide")
        squares = total[:, -128] + total[:, -1]
        scale = lax.rsqrt(squares / model_width + eps_norm)
        proj = (total[:, :-128] * scale[:, None]).reshape(slots, heads, QUERY_PER_KEY + 2, HEAD_WIDTH)
        angles = (slot_len + step).astype(jnp.float32)[:, None, None, None] * frequency
        turned = rotate(proj[:, :, : QUERY_PER_KEY + 1], jnp.cos(angles), jnp.sin(angles)).astype(
            jnp.bfloat16
        )
        queries = turned[:, :, :QUERY_PER_KEY]
        new_keys.append(turned[:, :, QUERY_PER_KEY])
        new_values.append(proj[:, :, QUERY_PER_KEY + 1].astype(jnp.bfloat16))
        fresh_keys, fresh_values = jnp.stack(new_keys, axis=2), jnp.stack(new_values, axis=2)
        all_keys = jnp.concatenate([keys, fresh_keys], axis=2)
        all_values = jnp.concatenate([values, fresh_values], axis=2)
        scores = (
            jnp.einsum("ngqd,ngkd->ngqk", queries, all_keys, preferred_element_type=jnp.float32)
            * score_scale
        )
        live = jnp.concatenate([valid, jnp.ones((slots, step + 1), bool)], axis=1)
        scores = jnp.where(live[:, None, None, :], scores, -1e30)
        weights = jnp.exp(scores - jnp.max(scores, axis=-1, keepdims=True))
        denominator = jnp.sum(weights, axis=-1, keepdims=True)
        summed = jnp.einsum(
            "ngqk,ngkd->ngqd",
            weights.astype(jnp.bfloat16),
            all_values,
            preferred_element_type=jnp.float32,
        )
        attended = (summed / denominator).astype(jnp.bfloat16).reshape(slots, -1)
        partial_rows = jnp.dot(attended, w_out, preferred_element_type=jnp.float32)
        state = (state_wide + exchange_sum(partial_rows.astype(jnp.bfloat16), "tp")).astype(
            jnp.bfloat16
        )
    return state, lax.dynamic_slice_in_dim(attended, me * own_cap, own_cap, axis=0)


def solution(mesh):
    in_specs = (
        P("grp", "wide"),
        P("wide"),
        P("wide", "tp"),
        P("tp", "wide"),
        P(("grp", "wide"), None, "tp"),
        P(("grp", "wide"), "tp", None),
        P("grp"),
        P("grp"),
    )
    out_specs = (P("grp", "wide"), P(("grp", "wide"), "tp"))
    return jax.shard_map(shards, mesh=mesh, in_specs=in_specs, out_specs=out_specs, check_vma=False)
```

time: 225 us -> 63.2 us (0.28)
  waiting for transfers between devices: 109 us -> 17.3 us
  blocking collectives: 65.1 us -> 0 us
  starting transfers between devices: 0.16 us -> 18.3 us
  between operations: 14.7 us -> 0.99 us
  matrix products: 24.6 us -> 20 us
  local copies, waits for them, and re-layouts: 4.93 us -> 1.62 us
    psum x2 -> x0, waiting for transfers between devices: 61.8 us -> none  [shards(): summed = lax.psum(partial_rows, 'tp')]
    unnamed x6 -> x0, waiting for transfers between devices: 47.3 us -> none
    all_gather x3 -> x0, blocking collectives: 40 us -> none  [the longest x2 26.3 us: shards(): lax.all_gather(attended, 'wide', axis=0, tiled=True)]
    psum x2 -> x0, blocking collectives: 25.1 us -> none  [shards(): squares = lax.psum(jnp.sum(state_wide * state_wide, axis=1), 'wide')]
    ppermute x0 -> x15, starting transfers between devices: none -> 18.3 us  [the longest x12 12.6 us: exchange_sum(): terms.append(lax.ppermute(partial, axis, pairs).astype(jnp.float32))]
    ppermute x0 -> x15, waiting for transfers between devices: none -> 17.3 us  [the longest x12 17.2 us: exchange_sum(): terms.append(lax.ppermute(partial, axis, pairs).astype(jnp.float32))]
    dot_general x12 -> x13, matrix products: 24.6 us -> 20 us  [the longest x2 9.31 us: shards(): partial_rows = jnp.dot(attended, w_out, preferred_element_type=jnp.float32)]
    unnamed x20 -> x18, local copies, waits for them, and re-layouts: 3.2 us -> 0.1 us
  transfers between devices with their start and end apart: 4 -> 15, of which waited for: 4 -> 9; matrix products, arithmetic and copies ran while one was open for 2% -> 16% of each run, Pallas kernels for 0% -> 0%
where the time goes in v1:
time: 63.2 us; the launch traced here: 62.9 us
  matrix products  20 us (32%)
  starting transfers between devices  18.3 us (29%)
  waiting for transfers between devices  17.3 us (27%)
  other arithmetic  4.81 us (8%)
  local copies, waits for them, and re-layouts  1.62 us (3%)
  between operations  0.99 us (2%)
    ppermute x12, waiting for transfers between devices, exchange_sum(): terms.append(lax.ppermute(partial, axis, pairs).astype(jnp.float32))  17.2 us
    ppermute x12, starting transfers between devices, exchange_sum(): terms.append(lax.ppermute(partial, axis, pairs).astype(jnp.float32))  12.6 us
    dot_general x2, matrix products, shards(): partial_rows = jnp.dot(attended, w_out, preferred_element_type=jnp.float32)  9.31 us
    dot_general x2, matrix products, shards(): jnp.dot((state_wide * gain).astype(jnp.bfloat16), query_key_value_weight,...  6.93 us
    ppermute x3, starting transfers between devices, exchange_gather(): blocks.append(lax.ppermute(block, axis, pairs))  5.71 us
    dot_general x1, matrix products, shards(): jnp.einsum('rgkp,rpgc->rgkc', pick, prompt_kv.reshape(requests_dev, lengt...  1.53 us
  transfers between devices with their start and end apart: 15, of which 9 were waited for; matrix products, arithmetic and copies ran while one was open for 16% of the time, Pallas kernels for 0%

profile of v1, /device:TPU:0, one launch (start us, length us, event | category | flops | bytes accessed | tf_op | source)
XLA Modules:
  0.0 62.9 jit_solution(14057609879087490970)
XLA Ops:
  0.7 1.5 %convolution_convert_fusion.4 = bf16[2,2,16,256]{3,2,1,0:T(8,128)(2,1)S(1)} fusion(bf16[2,64,2,8,256]{4,3,2,1,0:T(8,128)(2,1)} %bitcast.47, s32[2,2,16]{2,1,0:T(2,128)} %param.13), kind=kOutput, calls=%fused_computation.18 | convolution fusion | flops 16826368 | bytes 1081600 | tf_op jit(solution)/shard_map/rgkp,rpgc->rgkc/dot_general | solution.py:69
  2.2 5.1 %collective-permute-start.5 = (bf16[2,2,16,256]{3,2,1,0:T(8,128)(2,1)S(1)}, bf16[2,2,16,256]{3,2,1,0:T(8,128)(2,1)S(1)}, u32[]{:S(2)}, u32[]{:S(2)}) collective-permute-start(bf16[2,2,16,256]{3,2,1,0:T(8,128)(2,1)S(1)} %convolution_convert_fusion.4), channel_id=1, source_target_pairs={{0,12},{4,8},{8,4},{12,0},{1,13},{5,9},{9,5},{13,1},{2,14},{6,10},... | collective-permute-start | bytes 98312 | tf_op jit(solution)/shard_map/ppermute | solution.py:37
  7.3 0.6 %collective-permute-start.3 = (bf16[2,2,16,256]{3,2,1,0:T(8,128)(2,1)S(1)}, bf16[2,2,16,256]{3,2,1,0:T(8,128)(2,1)S(1)}, u32[]{:S(2)}, u32[]{:S(2)}) collective-permute-start(bf16[2,2,16,256]{3,2,1,0:T(8,128)(2,1)S(1)} %convolution_convert_fusion.4), channel_id=1, source_target_pairs={{0,4},{4,0},{8,12},{12,8},{1,5},{5,1},{9,13},{13,9},{2,6},{6,2},{1... | collective-permute-start | bytes 98312 | tf_op jit(solution)/shard_map/ppermute | solution.py:37
  7.9 1.0 %fusion.19 = f32[12]{0:T(128)S(1)} fusion(bf16[12,2048]{1,0:T(8,128)(2,1)} %param.8), kind=kLoop, calls=%fused_computation.48 | loop fusion | flops 73716 | bytes 49200 | tf_op jit(solution)/shard_map/reduce_sum | solution.py:107
  8.9 0.7 %convert_element_type.186 = f32[2048]{0:T(1024)S(1)} convert(bf16[2048]{0:T(1024)(128)(2,1)} %param.9) | non-fusion elementwise | flops 2048 | bytes 12288 | tf_op jit(solution)/shard_map/convert_element_type | solution.py:101
  9.6 5.5 %convolution_convert_fusion.1 = bf16[12,2560]{1,0:T(8,128)(2,1)S(1)} fusion(bf16[2048,2560]{1,0:T(8,128)(2,1)} %param.10, bf16[12,2048]{1,0:T(8,128)(2,1)} %param.8, f32[2048]{0:T(1024)S(1)} %convert_element_type.186), kind=kOutput, calls=%fused_computation.1 | convolution fusion | flops 125933568 | bytes 10604544 | tf_op jit(solution)/shard_map/dot_general | solution.py:110
  15.3 3.8 %collective-permute-start.2 = (bf16[12,2688]{1,0:T(8,128)(2,1)S(1)}, bf16[12,2688]{1,0:T(8,128)(2,1)S(1)}, u32[]{:S(2)}, u32[]{:S(2)}) collective-permute-start(bf16[12,2688]{1,0:T(8,128)(2,1)S(1)} %concatenate.33), channel_id=1, source_target_pairs={{0,12},{4,8},{8,4},{12,0},{1,13},{5,9},{9,5},{13,1},{2,14},{6,10},... | collective-permute-start | bytes 193544 | tf_op jit(solution)/shard_map/ppermute | solution.py:24
  20.0 0.7 %collective-permute-start = (bf16[12,2688]{1,0:T(8,128)(2,1)S(1)}, bf16[12,2688]{1,0:T(8,128)(2,1)S(1)}, u32[]{:S(2)}, u32[]{:S(2)}) collective-permute-start(bf16[12,2688]{1,0:T(8,128)(2,1)S(1)} %concatenate.33), channel_id=1, source_target_pairs={{0,4},{4,0},{8,12},{12,8},{1,5},{5,1},{9,13},{13,9},{2,6},{6,2},{1... | collective-permute-start | bytes 193544 | tf_op jit(solution)/shard_map/ppermute | solution.py:24
  22.1 3.5 %collective-permute-done.1 = bf16[12,2688]{1,0:T(8,128)(2,1)S(1)} collective-permute-done((bf16[12,2688]{1,0:T(8,128)(2,1)S(1)}, bf16[12,2688]{1,0:T(8,128)(2,1)S(1)}, u32[]{:S(2)}, u32[]{:S(2)}) %collective-permute-start.1) | collective-permute-done | bytes 64544 | tf_op jit(solution)/shard_map/ppermute | solution.py:24
  27.8 4.7 %convolution_convert_fusion.3 = bf16[12,2048]{1,0:T(8,128)(2,1)S(1)} fusion(bf16[12,2048]{1,0:T(8,128)(2,1)S(1)} %bitcast.44, bf16[2048,2048]{1,0:T(8,128)(2,1)} %param.11), kind=kOutput, calls=%fused_computation.3 | convolution fusion | flops 100687872 | bytes 8486912 | tf_op jit(solution)/shard_map/dot_general | solution.py:148
  32.5 1.5 %collective-permute-start.7 = (bf16[12,2048]{1,0:T(8,128)(2,1)S(1)}, bf16[12,2048]{1,0:T(8,128)(2,1)S(1)}, u32[]{:S(2)}, u32[]{:S(2)}) collective-permute-start(bf16[12,2048]{1,0:T(8,128)(2,1)S(1)} %convolution_convert_fusion.3), channel_id=1, source_target_pairs={{0,2},{1,3},{2,0},{3,1},{4,6},{5,7},{6,4},{7,5},{8,10},{9,11},{10,... | collective-permute-start | bytes 147464 | tf_op jit(solution)/shard_map/ppermute | solution.py:24
  34.4 2.5 %collective-permute-done.8 = bf16[12,2048]{1,0:T(8,128)(2,1)S(1)} collective-permute-done((bf16[12,2048]{1,0:T(8,128)(2,1)S(1)}, bf16[12,2048]{1,0:T(8,128)(2,1)S(1)}, u32[]{:S(2)}, u32[]{:S(2)}) %collective-permute-start.8) | collective-permute-done | bytes 49184 | tf_op jit(solution)/shard_map/ppermute | solution.py:24
  36.8 1.4 %collective-permute-done.7 = bf16[12,2048]{1,0:T(8,128)(2,1)S(1)} collective-permute-done((bf16[12,2048]{1,0:T(8,128)(2,1)S(1)}, bf16[12,2048]{1,0:T(8,128)(2,1)S(1)}, u32[]{:S(2)}, u32[]{:S(2)}) %collective-permute-start.7) | collective-permute-done | bytes 49184 | tf_op jit(solution)/shard_map/ppermute | solution.py:24
  38.5 1.5 %convolution_convert_fusion = bf16[12,2560]{1,0:T(8,128)(2,1)S(1)} fusion(bf16[2048,2560]{1,0:T(8,128)(2,1)S(1)} %bitcast.41, bf16[12,2048]{1,0:T(8,128)(2,1)S(1)} %get-tuple-element.3, f32[2048]{0:T(1024)S(1)} %convert_element_type.186), kind=kOutput, calls=%fused_computation | convolution fusion | flops 125933568 | bytes 10604544 | tf_op jit(solution)/shard_map/dot_general | solution.py:110
  40.2 2.1 %collective-permute-start.11 = (bf16[12,2688]{1,0:T(8,128)(2,1)S(1)}, bf16[12,2688]{1,0:T(8,128)(2,1)S(1)}, u32[]{:S(2)}, u32[]{:S(2)}) collective-permute-start(bf16[12,2688]{1,0:T(8,128)(2,1)S(1)} %concatenate.38), channel_id=1, source_target_pairs={{0,12},{4,8},{8,4},{12,0},{1,13},{5,9},{9,5},{13,1},{2,14},{6,10},... | collective-permute-start | bytes 193544 | tf_op jit(solution)/shard_map/ppermute | solution.py:24
  42.3 2.3 %collective-permute-start.9 = (bf16[12,2688]{1,0:T(8,128)(2,1)S(1)}, bf16[12,2688]{1,0:T(8,128)(2,1)S(1)}, u32[]{:S(2)}, u32[]{:S(2)}) collective-permute-start(bf16[12,2688]{1,0:T(8,128)(2,1)S(1)} %concatenate.38), channel_id=1, source_target_pairs={{0,4},{4,0},{8,12},{12,8},{1,5},{5,1},{9,13},{13,9},{2,6},{6,2},{1... | collective-permute-start | bytes 193544 | tf_op jit(solution)/shard_map/ppermute | solution.py:24
  44.6 2.9 %collective-permute-done.11 = bf16[12,2688]{1,0:T(8,128)(2,1)S(1)} collective-permute-done((bf16[12,2688]{1,0:T(8,128)(2,1)S(1)}, bf16[12,2688]{1,0:T(8,128)(2,1)S(1)}, u32[]{:S(2)}, u32[]{:S(2)}) %collective-permute-start.11) | collective-permute-done | bytes 64544 | tf_op jit(solution)/shard_map/ppermute | solution.py:24
  47.5 2.7 %collective-permute-done.10 = bf16[12,2688]{1,0:T(8,128)(2,1)S(1)} collective-permute-done((bf16[12,2688]{1,0:T(8,128)(2,1)S(1)}, bf16[12,2688]{1,0:T(8,128)(2,1)S(1)}, u32[]{:S(2)}, u32[]{:S(2)}) %collective-permute-start.10) | collective-permute-done | bytes 64544 | tf_op jit(solution)/shard_map/ppermute | solution.py:24
  51.9 4.6 %convolution_convert_fusion.2 = bf16[12,2048]{1,0:T(8,128)(2,1)S(1)} fusion(bf16[12,2048]{1,0:T(8,128)(2,1)S(1)} %bitcast.42, bf16[2048,2048]{1,0:T(8,128)(2,1)} %param.11), kind=kOutput, calls=%fused_computation.2 | convolution fusion | flops 100687872 | bytes 8486912 | tf_op jit(solution)/shard_map/dot_general | solution.py:148
  56.8 1.3 %collective-permute-start.13 = (bf16[12,2048]{1,0:T(8,128)(2,1)S(1)}, bf16[12,2048]{1,0:T(8,128)(2,1)S(1)}, u32[]{:S(2)}, u32[]{:S(2)}) collective-permute-start(bf16[12,2048]{1,0:T(8,128)(2,1)S(1)} %convolution_convert_fusion.2), channel_id=1, source_target_pairs={{0,2},{1,3},{2,0},{3,1},{4,6},{5,7},{6,4},{7,5},{8,10},{9,11},{10,... | collective-permute-start | bytes 147464 | tf_op jit(solution)/shard_map/ppermute | solution.py:24
  58.3 0.6 constant_dynamic-slice_fusion
  59.0 1.7 %collective-permute-done.14 = bf16[12,2048]{1,0:T(8,128)(2,1)S(1)} collective-permute-done((bf16[12,2048]{1,0:T(8,128)(2,1)S(1)}, bf16[12,2048]{1,0:T(8,128)(2,1)S(1)}, u32[]{:S(2)}, u32[]{:S(2)}) %collective-permute-start.14) | collective-permute-done | bytes 49184 | tf_op jit(solution)/shard_map/ppermute | solution.py:24
  60.7 1.6 %collective-permute-done.13 = bf16[12,2048]{1,0:T(8,128)(2,1)S(1)} collective-permute-done((bf16[12,2048]{1,0:T(8,128)(2,1)S(1)}, bf16[12,2048]{1,0:T(8,128)(2,1)S(1)}, u32[]{:S(2)}, u32[]{:S(2)}) %collective-permute-start.13) | collective-permute-done | bytes 49184 | tf_op jit(solution)/shard_map/ppermute | solution.py:24
  62.3 0.7 %fusion.23 = bf16[12,2048]{1,0:T(8,128)(2,1)} fusion(bf16[12,2048]{1,0:T(8,128)(2,1)S(1)} %get-tuple-element.3, bf16[12,2048]{1,0:T(8,128)(2,1)S(1)} %collective-permute-done.14, bf16[12,2048]{1,0:T(8,128)(2,1)S(1)} %collective-permute-done.13, bf16[12,2048]{1,0:T(8,128)(2,1)S(1)} %collective-permute-done.12, bf16[12,2048]{1,0:T(8,128)(2,1)S(1)} %convolution_convert_fusion.2), kind=kLoop, calls=%fused_computation.52 | loop fusion | flops 245760 | bytes 294912 | tf_op jit(solution)/shard_map/convert_element_type | solution.py:149
  (86 shorter events, 7.5 us)
Async XLA Ops:
  0.6 18.4 %copy-start.1 = (s32[8]{0:T(128)S(1)}, s32[8]{0:T(128)}, u32[]{:S(2)}) copy-start(s32[8]{0:T(128)} %param.14) | copy-start | bytes 100
  0.6 18.7 %copy-start.2 = (s32[8]{0:T(128)S(1)}, s32[8]{0:T(128)}, u32[]{:S(2)}) copy-start(s32[8]{0:T(128)} %param.15) | copy-start | bytes 100
  2.2 18.8 %collective-permute-start.5 = (bf16[2,2,16,256]{3,2,1,0:T(8,128)(2,1)S(1)}, bf16[2,2,16,256]{3,2,1,0:T(8,128)(2,1)S(1)}, u32[]{:S(2)}, u32[]{:S(2)}) collective-permute-start(bf16[2,2,16,256]{3,2,1,0:T(8,128)(2,1)S(1)} %convolution_convert_fusion.4), channel_id=1, source_target_pairs={{0,12},{4,8},{8,4},{12,0},{1,13},{5,9},{9,5},{13,1},{2,14},{6,10},... | collective-permute-start | bytes 98312 | tf_op jit(solution)/shard_map/ppermute | solution.py:37
  7.3 14.0 %collective-permute-start.4 = (bf16[2,2,16,256]{3,2,1,0:T(8,128)(2,1)S(1)}, bf16[2,2,16,256]{3,2,1,0:T(8,128)(2,1)S(1)}, u32[]{:S(2)}, u32[]{:S(2)}) collective-permute-start(bf16[2,2,16,256]{3,2,1,0:T(8,128)(2,1)S(1)} %convolution_convert_fusion.4), channel_id=1, source_target_pairs={{0,8},{4,12},{8,0},{12,4},{1,9},{5,13},{9,1},{13,5},{2,10},{6,14},... | collective-permute-start | bytes 98312 | tf_op jit(solution)/shard_map/ppermute | solution.py:37
  7.3 12.7 %collective-permute-start.3 = (bf16[2,2,16,256]{3,2,1,0:T(8,128)(2,1)S(1)}, bf16[2,2,16,256]{3,2,1,0:T(8,128)(2,1)S(1)}, u32[]{:S(2)}, u32[]{:S(2)}) collective-permute-start(bf16[2,2,16,256]{3,2,1,0:T(8,128)(2,1)S(1)} %convolution_convert_fusion.4), channel_id=1, source_target_pairs={{0,4},{4,0},{8,12},{12,8},{1,5},{5,1},{9,13},{13,9},{2,6},{6,2},{1... | collective-permute-start | bytes 98312 | tf_op jit(solution)/shard_map/ppermute | solution.py:37
  15.3 6.8 %collective-permute-start.2 = (bf16[12,2688]{1,0:T(8,128)(2,1)S(1)}, bf16[12,2688]{1,0:T(8,128)(2,1)S(1)}, u32[]{:S(2)}, u32[]{:S(2)}) collective-permute-start(bf16[12,2688]{1,0:T(8,128)(2,1)S(1)} %concatenate.33), channel_id=1, source_target_pairs={{0,12},{4,8},{8,4},{12,0},{1,13},{5,9},{9,5},{13,1},{2,14},{6,10},... | collective-permute-start | bytes 193544 | tf_op jit(solution)/shard_map/ppermute | solution.py:24
  19.0 6.5 %collective-permute-start.1 = (bf16[12,2688]{1,0:T(8,128)(2,1)S(1)}, bf16[12,2688]{1,0:T(8,128)(2,1)S(1)}, u32[]{:S(2)}, u32[]{:S(2)}) collective-permute-start(bf16[12,2688]{1,0:T(8,128)(2,1)S(1)} %concatenate.33), channel_id=1, source_target_pairs={{0,8},{4,12},{8,0},{12,4},{1,9},{5,13},{9,1},{13,5},{2,10},{6,14},... | collective-permute-start | bytes 193544 | tf_op jit(solution)/shard_map/ppermute | solution.py:24
  20.0 6.0 %collective-permute-start = (bf16[12,2688]{1,0:T(8,128)(2,1)S(1)}, bf16[12,2688]{1,0:T(8,128)(2,1)S(1)}, u32[]{:S(2)}, u32[]{:S(2)}) collective-permute-start(bf16[12,2688]{1,0:T(8,128)(2,1)S(1)} %concatenate.33), channel_id=1, source_target_pairs={{0,4},{4,0},{8,12},{12,8},{1,5},{5,1},{9,13},{13,9},{2,6},{6,2},{1... | collective-permute-start | bytes 193544 | tf_op jit(solution)/shard_map/ppermute | solution.py:24
  26.2 12.1 %copy-start = (bf16[12,2048]{1,0:T(8,128)(2,1)S(1)}, bf16[12,2048]{1,0:T(8,128)(2,1)}, u32[]{:S(2)}) copy-start(bf16[12,2048]{1,0:T(8,128)(2,1)} %param.8) | copy-start | bytes 147460
  26.4 12.1 %slice-start = ((s8[10485760]{0:T(1024)(128)(4,1)}), s8[4194304]{0:T(1024)(128)(4,1)S(1)}, s32[]{:S(2)}) async-start(s8[10485760]{0:T(1024)(128)(4,1)} %bitcast.40), calls=%async_computation | async-start | bytes 8388608
  27.7 10.8 %slice-start.1 = ((s8[10485760]{0:T(1024)(128)(4,1)}), s8[4194304]{0:T(1024)(128)(4,1)S(1)}, s32[]{:S(2)}) async-start(s8[10485760]{0:T(1024)(128)(4,1)} %bitcast.40), calls=%async_computation.1 | async-start | bytes 8388608
  27.7 10.7 %slice-start.2 = ((s8[10485760]{0:T(1024)(128)(4,1)}), s8[2097152]{0:T(1024)(128)(4,1)S(1)}, s32[]{:S(2)}) async-start(s8[10485760]{0:T(1024)(128)(4,1)} %bitcast.40), calls=%async_computation.2 | async-start | bytes 4194304
  32.5 4.4 %collective-permute-start.8 = (bf16[12,2048]{1,0:T(8,128)(2,1)S(1)}, bf16[12,2048]{1,0:T(8,128)(2,1)S(1)}, u32[]{:S(2)}, u32[]{:S(2)}) collective-permute-start(bf16[12,2048]{1,0:T(8,128)(2,1)S(1)} %convolution_convert_fusion.3), channel_id=1, source_target_pairs={{0,3},{1,2},{2,1},{3,0},{4,7},{5,6},{6,5},{7,4},{8,11},{9,10},{10,... | collective-permute-start | bytes 147464 | tf_op jit(solution)/shard_map/ppermute | solution.py:24
  32.5 5.8 %collective-permute-start.7 = (bf16[12,2048]{1,0:T(8,128)(2,1)S(1)}, bf16[12,2048]{1,0:T(8,128)(2,1)S(1)}, u32[]{:S(2)}, u32[]{:S(2)}) collective-permute-start(bf16[12,2048]{1,0:T(8,128)(2,1)S(1)} %convolution_convert_fusion.3), channel_id=1, source_target_pairs={{0,2},{1,3},{2,0},{3,1},{4,6},{5,7},{6,4},{7,5},{8,10},{9,11},{10,... | collective-permute-start | bytes 147464 | tf_op jit(solution)/shard_map/ppermute | solution.py:24
  34.0 4.3 %collective-permute-start.6 = (bf16[12,2048]{1,0:T(8,128)(2,1)S(1)}, bf16[12,2048]{1,0:T(8,128)(2,1)S(1)}, u32[]{:S(2)}, u32[]{:S(2)}) collective-permute-start(bf16[12,2048]{1,0:T(8,128)(2,1)S(1)} %convolution_convert_fusion.3), channel_id=1, source_target_pairs={{0,1},{1,0},{2,3},{3,2},{4,5},{5,4},{6,7},{7,6},{8,9},{9,8},{10,11... | collective-permute-start | bytes 147464 | tf_op jit(solution)/shard_map/ppermute | solution.py:24
  40.2 7.3 %collective-permute-start.11 = (bf16[12,2688]{1,0:T(8,128)(2,1)S(1)}, bf16[12,2688]{1,0:T(8,128)(2,1)S(1)}, u32[]{:S(2)}, u32[]{:S(2)}) collective-permute-start(bf16[12,2688]{1,0:T(8,128)(2,1)S(1)} %concatenate.38), channel_id=1, source_target_pairs={{0,12},{4,8},{8,4},{12,0},{1,13},{5,9},{9,5},{13,1},{2,14},{6,10},... | collective-permute-start | bytes 193544 | tf_op jit(solution)/shard_map/ppermute | solution.py:24
  42.3 7.9 %collective-permute-start.10 = (bf16[12,2688]{1,0:T(8,128)(2,1)S(1)}, bf16[12,2688]{1,0:T(8,128)(2,1)S(1)}, u32[]{:S(2)}, u32[]{:S(2)}) collective-permute-start(bf16[12,2688]{1,0:T(8,128)(2,1)S(1)} %concatenate.38), channel_id=1, source_target_pairs={{0,8},{4,12},{8,0},{12,4},{1,9},{5,13},{9,1},{13,5},{2,10},{6,14},... | collective-permute-start | bytes 193544 | tf_op jit(solution)/shard_map/ppermute | solution.py:24
  42.3 7.9 %collective-permute-start.9 = (bf16[12,2688]{1,0:T(8,128)(2,1)S(1)}, bf16[12,2688]{1,0:T(8,128)(2,1)S(1)}, u32[]{:S(2)}, u32[]{:S(2)}) collective-permute-start(bf16[12,2688]{1,0:T(8,128)(2,1)S(1)} %concatenate.38), channel_id=1, source_target_pairs={{0,4},{4,0},{8,12},{12,8},{1,5},{5,1},{9,13},{13,9},{2,6},{6,2},{1... | collective-permute-start | bytes 193544 | tf_op jit(solution)/shard_map/ppermute | solution.py:24
  56.5 4.2 %collective-permute-start.14 = (bf16[12,2048]{1,0:T(8,128)(2,1)S(1)}, bf16[12,2048]{1,0:T(8,128)(2,1)S(1)}, u32[]{:S(2)}, u32[]{:S(2)}) collective-permute-start(bf16[12,2048]{1,0:T(8,128)(2,1)S(1)} %convolution_convert_fusion.2), channel_id=1, source_target_pairs={{0,3},{1,2},{2,1},{3,0},{4,7},{5,6},{6,5},{7,4},{8,11},{9,10},{10,... | collective-permute-start | bytes 147464 | tf_op jit(solution)/shard_map/ppermute | solution.py:24
  56.8 5.5 %collective-permute-start.13 = (bf16[12,2048]{1,0:T(8,128)(2,1)S(1)}, bf16[12,2048]{1,0:T(8,128)(2,1)S(1)}, u32[]{:S(2)}, u32[]{:S(2)}) collective-permute-start(bf16[12,2048]{1,0:T(8,128)(2,1)S(1)} %convolution_convert_fusion.2), channel_id=1, source_target_pairs={{0,2},{1,3},{2,0},{3,1},{4,6},{5,7},{6,4},{7,5},{8,10},{9,11},{10,... | collective-permute-start | bytes 147464 | tf_op jit(solution)/shard_map/ppermute | solution.py:24
  58.1 4.2 %collective-permute-start.12 = (bf16[12,2048]{1,0:T(8,128)(2,1)S(1)}, bf16[12,2048]{1,0:T(8,128)(2,1)S(1)}, u32[]{:S(2)}, u32[]{:S(2)}) collective-permute-start(bf16[12,2048]{1,0:T(8,128)(2,1)S(1)} %convolution_convert_fusion.2), channel_id=1, source_target_pairs={{0,1},{1,0},{2,3},{3,2},{4,5},{5,4},{6,7},{7,6},{8,9},{9,8},{10,11... | collective-permute-start | bytes 147464 | tf_op jit(solution)/shard_map/ppermute | solution.py:24

commit v2 on v1

--- a/solution.py
+++ b/solution.py
@@ -14,28 +14,18 @@
 eps_norm = 1e-05
 
 
-def exchange_sum(partial, axis):
-    count = lax.axis_size(axis)
-    if count > DIRECT_LIMIT:
-        return lax.psum(partial.astype(jnp.float32), axis)
-    terms = [partial.astype(jnp.float32)]
-    for offset in range(1, count):
-        pairs = [(i, i ^ offset) for i in range(count)]
-        terms.append(lax.ppermute(partial, axis, pairs).astype(jnp.float32))
-    while len(terms) > 1:
-        terms = [terms[i] + terms[i + 1] for i in range(0, len(terms), 2)]
-    return terms[0]
-
-
 def exchange_gather(block, axis):
     count = lax.axis_size(axis)
     if count > DIRECT_LIMIT:
-        return lax.all_gather(block, axis, axis=0, tiled=True)
-    blocks = [block]
-    for offset in range(1, count):
-        pairs = [(i, i ^ offset) for i in range(count)]
-        blocks.append(lax.ppermute(block, axis, pairs))
-    return blocks
+        return lax.all_gather(block, axis, axis=0)
+    copies = jnp.broadcast_to(block[None], (count,) + block.shape)
+    return lax.all_to_all(copies, axis, split_axis=0, concat_axis=0)
+
+
+def exchange_sum(partial, axis):
+    if lax.axis_size(axis) > DIRECT_LIMIT:
+        return lax.psum(partial.astype(jnp.float32), axis)
+    return jnp.sum(exchange_gather(partial, axis).astype(jnp.float32), axis=0)
 
 
 def rotate(vector, cosine, sine):
@@ -73,25 +63,13 @@
         preferred_element_type=jnp.float32,
     ).astype(jnp.bfloat16)
     blocks = exchange_gather(kept, "wide")
-    if isinstance(blocks, list):
-        cache = 0.0
-        for offset, block in enumerate(blocks):
-            source = me ^ offset
-            columns = lax.dynamic_slice_in_dim(matches, source * requests_dev, requests_dev, axis=1)
-            cache = cache + jnp.einsum(
-                "sr,rgkc->sgkc",
-                columns.astype(jnp.bfloat16),
-                block,
-                preferred_element_type=jnp.float32,
-            )
-        cache = cache.astype(jnp.bfloat16)
-    else:
-        cache = jnp.einsum(
-            "sr,rgkc->sgkc",
-            matches.astype(jnp.bfloat16),
-            blocks,
-            preferred_element_type=jnp.float32,
-        ).astype(jnp.bfloat16)
+    blocks = blocks.reshape((requests,) + kept.shape[1:])
+    cache = jnp.einsum(
+        "sr,rgkc->sgkc",
+        matches.astype(jnp.bfloat16),
+        blocks,
+        preferred_element_type=jnp.float32,
+    ).astype(jnp.bfloat16)
     keys, values = cache[..., :HEAD_WIDTH], cache[..., HEAD_WIDTH:]
     valid = jnp.arange(kept_positions, dtype=jnp.int32)[None, :] < slot_len[:, None]
     score_scale = 1.0 / math.sqrt(HEAD_WIDTH)

time: 63.2 us -> 84.7 us (1.34)
  blocking collectives: 0 us -> 8.6 us
  waiting for transfers between devices: 17.3 us -> 25.4 us
  local copies, waits for them, and re-layouts: 1.62 us -> 4.76 us
  other arithmetic: 4.81 us -> 6.84 us
    all_to_all x0 -> x4, waiting for transfers between devices: none -> 25.4 us  [exchange_gather(): return lax.all_to_all(copies, axis, split_axis=0, concat_axis=0)]
    ppermute x15 -> x0, starting transfers between devices: 18.3 us -> none  [the longest x12 12.6 us: exchange_sum(): terms.append(lax.ppermute(partial, axis, pairs).astype(jnp.float32))]
    all_to_all x0 -> x4, starting transfers between devices: none -> 18.3 us  [exchange_gather(): return lax.all_to_all(copies, axis, split_axis=0, concat_axis=0)]
    ppermute x15 -> x0, waiting for transfers between devices: 17.3 us -> none  [the longest x12 17.2 us: exchange_sum(): terms.append(lax.ppermute(partial, axis, pairs).astype(jnp.float32))]
    all_to_all x0 -> x1, blocking collectives: none -> 8.6 us  [exchange_gather(): return lax.all_to_all(copies, axis, split_axis=0, concat_axis=0)]
    broadcast_in_dim x0 -> x5, local copies, waits for them, and re-layouts: none -> 2.94 us  [exchange_gather(): copies = jnp.broadcast_to(block[None], (count,) + block.shape)]
  transfers between devices with their start and end apart: 15 -> 4, of which waited for: 9 -> 3; matrix products, arithmetic and copies ran while one was open for 16% -> 13% of each run, Pallas kernels for 0% -> 0%
where the time goes in v2:
time: 84.7 us; the launch traced here: 84 us
  waiting for transfers between devices  25.4 us (30%)
  matrix products  19.2 us (23%)
  starting transfers between devices  18.3 us (22%)
  blocking collectives  8.6 us (10%)
  other arithmetic  6.84 us (8%)
  local copies, waits for them, and re-layouts  4.76 us (6%)
  between operations  0.99 us (1%)
    all_to_all x4, waiting for transfers between devices, exchange_gather(): return lax.all_to_all(copies, axis, split_axis=0, concat_axis=0)  25.4 us
    all_to_all x4, starting transfers between devices, exchange_gather(): return lax.all_to_all(copies, axis, split_axis=0, concat_axis=0)  18.3 us
    dot_general x2, matrix products, shards(): partial_rows = jnp.dot(attended, w_out, preferred_element_type=jnp.float32)  9.31 us
    all_to_all x1, blocking collectives, exchange_gather(): return lax.all_to_all(copies, axis, split_axis=0, concat_axis=0)  8.6 us
    dot_general x2, matrix products, shards(): jnp.dot((state_wide * gain).astype(jnp.bfloat16), query_key_value_weight,...  6.93 us
    broadcast_in_dim x5, local copies, waits for them, and re-layouts, exchange_gather(): copies = jnp.broadcast_to(block[None], (count,) + block.shape)  2.94 us
  transfers between devices with their start and end apart: 4, of which 3 were waited for; matrix products, arithmetic and copies ran while one was open for 13% of the time, Pallas kernels for 0%

profile of v2, /device:TPU:0, one launch (start us, length us, event | category | flops | bytes accessed | tf_op | source)
XLA Modules:
  0.0 84.0 jit_solution(13339506402665660537)
XLA Ops:
  0.6 1.5 %convolution_convert_fusion.5 = bf16[2,2,16,256]{3,2,1,0:T(8,128)(2,1)S(1)} fusion(bf16[2,64,2,8,256]{4,3,2,1,0:T(8,128)(2,1)} %bitcast.35, s32[2,2,16]{2,1,0:T(2,128)} %param.13), kind=kOutput, calls=%fused_computation.15 | convolution fusion | flops 16826368 | bytes 1081600 | tf_op jit(solution)/shard_map/rgkp,rpgc->rgkc/dot_general | solution.py:59
  2.2 0.7 broadcast_in_dim.56
  2.9 6.3 %all-to-all-start.1 = ((bf16[4,2,2,16,256]{4,1,3,2,0:T(2,128)(2,1)}), bf16[4,2,2,16,256]{4,1,3,2,0:T(2,128)(2,1)S(1)}, u32[]{:S(2)}, u32[]{:S(2)}) async-start(bf16[4,2,2,16,256]{4,1,3,2,0:T(2,128)(2,1)} %broadcast_in_dim.56), calls=%async_computation.1 | async-start | bytes 262144 | tf_op jit(solution)/shard_map/all_to_all | solution.py:22
  9.2 0.9 %convert_reduce_fusion.4 = s32[8]{0:T(128)S(1)} fusion(s32[8]{0:T(128)} %param.14), kind=kLoop, calls=%fused_computation.91 | loop fusion | flops 312 | bytes 64 | tf_op jit(solution)/shard_map/reduce_sum | solution.py:51
  10.2 0.7 multiply_add_fusion
  10.8 0.7 select_reduce_fusion
  11.6 1.0 %fusion.17 = f32[12]{0:T(128)S(1)} fusion(bf16[12,2048]{1,0:T(8,128)(2,1)} %param.8), kind=kLoop, calls=%fused_computation.47 | loop fusion | flops 73716 | bytes 49200 | tf_op jit(solution)/shard_map/reduce_sum | solution.py:85
  12.6 0.7 convert_element_type.147
  13.3 5.5 %convolution_convert_fusion.1 = bf16[12,2560]{1,0:T(8,128)(2,1)S(1)} fusion(bf16[2048,2560]{1,0:T(8,128)(2,1)} %param.10, bf16[12,2048]{1,0:T(8,128)(2,1)} %param.8, f32[2048]{0:T(1024)S(1)} %convert_element_type.147), kind=kOutput, calls=%fused_computation.1 | convolution fusion | flops 125933568 | bytes 10604544 | tf_op jit(solution)/shard_map/dot_general | solution.py:88
  19.2 0.7 broadcast_in_dim.55
  19.9 5.1 %all-to-all-start = ((bf16[4,12,2688]{2,1,0:T(8,128)(2,1)}), bf16[4,12,2688]{2,1,0:T(8,128)(2,1)S(1)}, u32[]{:S(2)}, u32[]{:S(2)}) async-start(bf16[4,12,2688]{2,1,0:T(8,128)(2,1)} %broadcast_in_dim.55), calls=%async_computation | async-start | bytes 688128 | tf_op jit(solution)/shard_map/all_to_all | solution.py:22
  25.6 9.5 %all-to-all-done = bf16[4,12,2688]{2,1,0:T(8,128)(2,1)S(1)} async-done(((bf16[4,12,2688]{2,1,0:T(8,128)(2,1)}), bf16[4,12,2688]{2,1,0:T(8,128)(2,1)S(1)}, u32[]{:S(2)}, u32[]{:S(2)}) %all-to-all-start) | async-done | bytes 258080 | tf_op jit(solution)/shard_map/all_to_all | solution.py:22
  36.9 4.7 %convolution_convert_fusion.3 = bf16[12,2048]{1,0:T(8,128)(2,1)S(1)} fusion(bf16[12,2048]{1,0:T(8,128)(2,1)S(1)} %bitcast.32, bf16[2048,2048]{1,0:T(8,128)(2,1)} %param.11), kind=kOutput, calls=%fused_computation.3 | convolution fusion | flops 100687872 | bytes 8486912 | tf_op jit(solution)/shard_map/dot_general | solution.py:126
  41.6 8.6 %all_to_all.25 = bf16[4,12,2048]{2,1,0:T(8,128)(2,1)S(1)} all-to-all(bf16[4,12,2048]{2,1,0:T(8,128)(2,1)S(1)} %broadcast_in_dim.58), channel_id=1, replica_groups=mesh['grp'=2,'wide'=4,'tp'=4] {'tp'}, dimensions={0} | all-to-all | bytes 393216 | tf_op jit(solution)/shard_map/all_to_all | solution.py:22
  50.5 1.5 %convolution_convert_fusion = bf16[12,2560]{1,0:T(8,128)(2,1)S(1)} fusion(bf16[2048,2560]{1,0:T(8,128)(2,1)S(1)} %bitcast.29, bf16[12,2048]{1,0:T(8,128)(2,1)S(1)} %get-tuple-element.3, f32[2048]{0:T(1024)S(1)} %convert_element_type.147), kind=kOutput, calls=%fused_computation | convolution fusion | flops 125933568 | bytes 10604544 | tf_op jit(solution)/shard_map/dot_general | solution.py:88
  52.2 0.8 broadcast_in_dim.62
  52.9 3.5 %all-to-all-start.3 = ((bf16[4,12,2688]{2,1,0:T(8,128)(2,1)}), bf16[4,12,2688]{2,1,0:T(8,128)(2,1)S(1)}, u32[]{:S(2)}, u32[]{:S(2)}) async-start(bf16[4,12,2688]{2,1,0:T(8,128)(2,1)} %broadcast_in_dim.62), calls=%async_computation.3 | async-start | bytes 688128 | tf_op jit(solution)/shard_map/all_to_all | solution.py:22
  56.4 10.5 %all-to-all-done.3 = bf16[4,12,2688]{2,1,0:T(8,128)(2,1)S(1)} async-done(((bf16[4,12,2688]{2,1,0:T(8,128)(2,1)}), bf16[4,12,2688]{2,1,0:T(8,128)(2,1)S(1)}, u32[]{:S(2)}, u32[]{:S(2)}) %all-to-all-start.3) | async-done | bytes 258080 | tf_op jit(solution)/shard_map/all_to_all | solution.py:22
  68.6 4.6 %convolution_convert_fusion.2 = bf16[12,2048]{1,0:T(8,128)(2,1)S(1)} fusion(bf16[12,2048]{1,0:T(8,128)(2,1)S(1)} %bitcast.30, bf16[2048,2048]{1,0:T(8,128)(2,1)} %param.11), kind=kOutput, calls=%fused_computation.2 | convolution fusion | flops 100687872 | bytes 8486912 | tf_op jit(solution)/shard_map/dot_general | solution.py:126
  73.2 0.7 broadcast_in_dim.64
  73.9 3.4 %all-to-all-start.4 = ((bf16[4,12,2048]{2,1,0:T(8,128)(2,1)}), bf16[4,12,2048]{2,1,0:T(8,128)(2,1)S(1)}, u32[]{:S(2)}, u32[]{:S(2)}) async-start(bf16[4,12,2048]{2,1,0:T(8,128)(2,1)} %broadcast_in_dim.64), calls=%async_computation.4 | async-start | bytes 524288 | tf_op jit(solution)/shard_map/all_to_all | solution.py:22
  77.3 0.6 constant_dynamic-slice_fusion
  77.9 5.4 %all-to-all-done.4 = bf16[4,12,2048]{2,1,0:T(8,128)(2,1)S(1)} async-done(((bf16[4,12,2048]{2,1,0:T(8,128)(2,1)}), bf16[4,12,2048]{2,1,0:T(8,128)(2,1)S(1)}, u32[]{:S(2)}, u32[]{:S(2)}) %all-to-all-start.4) | async-done | bytes 196640 | tf_op jit(solution)/shard_map/all_to_all | solution.py:22
  83.4 0.6 fusion.21
  (67 shorter events, 4.8 us)
Async XLA Ops:
  2.9 16.3 %all-to-all-start.1 = ((bf16[4,2,2,16,256]{4,1,3,2,0:T(2,128)(2,1)}), bf16[4,2,2,16,256]{4,1,3,2,0:T(2,128)(2,1)S(1)}, u32[]{:S(2)}, u32[]{:S(2)}) async-start(bf16[4,2,2,16,256]{4,1,3,2,0:T(2,128)(2,1)} %broadcast_in_dim.56), calls=%async_computation.1 | async-start | bytes 262144 | tf_op jit(solution)/shard_map/all_to_all | solution.py:22
  19.9 15.2 %all-to-all-start = ((bf16[4,12,2688]{2,1,0:T(8,128)(2,1)}), bf16[4,12,2688]{2,1,0:T(8,128)(2,1)S(1)}, u32[]{:S(2)}, u32[]{:S(2)}) async-start(bf16[4,12,2688]{2,1,0:T(8,128)(2,1)} %broadcast_in_dim.55), calls=%async_computation | async-start | bytes 688128 | tf_op jit(solution)/shard_map/all_to_all | solution.py:22
  35.6 14.7 %copy-start = (bf16[12,2048]{1,0:T(8,128)(2,1)S(1)}, bf16[12,2048]{1,0:T(8,128)(2,1)}, u32[]{:S(2)}) copy-start(bf16[12,2048]{1,0:T(8,128)(2,1)} %param.8) | copy-start | bytes 147460
  35.6 14.8 %slice-start = ((s8[10485760]{0:T(1024)(128)(4,1)}), s8[4194304]{0:T(1024)(128)(4,1)S(1)}, s32[]{:S(2)}) async-start(s8[10485760]{0:T(1024)(128)(4,1)} %bitcast.28), calls=%async_computation.5 | async-start | bytes 8388608
  36.9 13.6 %slice-start.1 = ((s8[10485760]{0:T(1024)(128)(4,1)}), s8[4194304]{0:T(1024)(128)(4,1)S(1)}, s32[]{:S(2)}) async-start(s8[10485760]{0:T(1024)(128)(4,1)} %bitcast.28), calls=%async_computation.6 | async-start | bytes 8388608
  36.9 13.6 %slice-start.2 = ((s8[10485760]{0:T(1024)(128)(4,1)}), s8[2097152]{0:T(1024)(128)(4,1)S(1)}, s32[]{:S(2)}) async-start(s8[10485760]{0:T(1024)(128)(4,1)} %bitcast.28), calls=%async_computation.7 | async-start | bytes 4194304
  52.9 14.0 %all-to-all-start.3 = ((bf16[4,12,2688]{2,1,0:T(8,128)(2,1)}), bf16[4,12,2688]{2,1,0:T(8,128)(2,1)S(1)}, u32[]{:S(2)}, u32[]{:S(2)}) async-start(bf16[4,12,2688]{2,1,0:T(8,128)(2,1)} %broadcast_in_dim.62), calls=%async_computation.3 | async-start | bytes 688128 | tf_op jit(solution)/shard_map/all_to_all | solution.py:22
  73.9 9.4 %all-to-all-start.4 = ((bf16[4,12,2048]{2,1,0:T(8,128)(2,1)}), bf16[4,12,2048]{2,1,0:T(8,128)(2,1)S(1)}, u32[]{:S(2)}, u32[]{:S(2)}) async-start(bf16[4,12,2048]{2,1,0:T(8,128)(2,1)} %broadcast_in_dim.64), calls=%async_computation.4 | async-start | bytes 524288 | tf_op jit(solution)/shard_map/all_to_all | solution.py:22
